TPU v7x, 32 devices: a whole 2x2x4 slice. The times are simulated.
32 devices in a mesh: harm: 4 (over z), node: 8 (over y, x, core).
Axes of the slice: x: 2, y: 2, z: 4, core: 2. Of those that a mesh axis runs over, the one named last changes fastest.
Arguments:
- adjoint: bfloat16 [128, 4, 32768], P('harm', None, 'node'), may hold values from -6 to 6
- source: float32 [128, 131072], P(None, ('harm', 'node')), may hold values from -6 to 6
- rad_coeff: bfloat16 [128, 131072], P(None, ('harm', 'node')), may hold values from 0.19921875 to 2
- capacity: float32 [131072], P(('harm', 'node')), may hold values from 0.005 to 0.03
- inv_diag: float32 [131072], P(('harm', 'node')), may hold values from 0.1 to 0.5
- blocks: bfloat16 [1024, 4, 128, 128], P(('harm', 'node')), may hold values from -0.25 to 0.25
- block_cols: int32 [1024, 4], P(('harm', 'node')), may hold values from 0 to 1023, as said below
- zone_of: int32 [131072], P(('harm', 'node')), may hold values from 0 to 1279, as said below
- heater_weight: float32 [131072], P(('harm', 'node')), may hold values from 0.2 to 2
Outputs:
- updated: bfloat16 [128, 4, 32768], P('harm', None, 'node')
- gradient: float32 [1280, 128], P(('harm', 'node'))
Inputs may be any that keep to these rules, and one draw needn't show every extreme that they name: `block_cols`: with d = b // 32 and D = 32: slot 0 of row block b names b itself; slot 1 lies in row blocks max(d - 1, 0) * 32 to (max(d - 1, 0) + 1) * 32 - 1; slot 2 in min(d + 1, D - 1) * 32 to (min(d + 1, D - 1) + 1) * 32 - 1; the other slots in (d - 1) * 32 to (d + 2) * 32 - 1. `zone_of`: node n lies in a zone z with (n // 4096 - 1) * 40 <= z < (n // 4096 + 2) * 40.
All inputs are finite; a program needn't handle non-finite values.
Results may differ from a plain program's by a relative error of at most 0.0035.
Values may be sent and summed in bfloat16 or wider, within the bound.
A program may use at most 64 MiB of HBM per device.

v0:
```python
import math
import jax
import jax.numpy as jnp
from jax import lax
from jax.sharding import PartitionSpec as P

ZONE_DEV = 40


def with_halo(value, sides, width):
    for axis, dim in sides:
        count, length = (lax.axis_size(axis), value.shape[dim])
        up = [(i, (i + 1) % count) for i in range(count - 1)]
        down = [(j, i) for i, j in up]
        last = lax.slice_in_dim(value, length - width, length, axis=dim)
        initial = lax.slice_in_dim(value, 0, width, axis=dim)
        before = lax.ppermute(last, axis, up)
        after = lax.ppermute(initial, axis, down)
        value = jnp.concatenate([before, value, after], axis=dim)
    return value


def passed_along(value, axis, steps):
    count = lax.axis_size(axis)
    initial, last = (max(0, -steps), min(count, count - steps))
    return lax.ppermute(value, axis, [(source, source + steps) for source in range(initial, last)])


def fourier_basis(count):
    sample_index = jnp.arange(count, dtype=jnp.float32)[:, None]
    column_index = jnp.arange(count)[None, :]
    half_count = count // 2
    frequency = jnp.where(
        column_index <= half_count, column_index, column_index - half_count
    ).astype(jnp.float32)
    angle = 2.0 * math.pi * frequency * sample_index / count
    values_table = jnp.where(column_index <= half_count, jnp.cos(angle), jnp.sin(angle))
    scaling = jnp.where(
        (column_index == 0) | (column_index == half_count),
        math.sqrt(1.0 / count),
        math.sqrt(2.0 / count),
    )
    return (values_table * scaling).astype(jnp.bfloat16)


def derivative_term(field):
    half_count = field.shape[0] // 2
    wave_number = jnp.arange(1, half_count, dtype=jnp.float32)[:, None]
    zero_row = jnp.zeros((1, field.shape[1]), jnp.float32)
    upper_rows = wave_number * field[half_count + 1 :]
    lower_rows = -wave_number * field[1:half_count]
    return jnp.concatenate([zero_row, upper_rows, zero_row, lower_rows], axis=0)


def body(
    adjoint, source, rad_coeff, capacity, inv_diag, blocks, block_cols, zone_of, heater_weight
):
    arrived = lax.all_to_all(adjoint, "harm", split_axis=1, concat_axis=0, tiled=True)
    harmonics = arrived.shape[0]
    node_count = arrived.shape[2]
    field = arrived.reshape(harmonics, node_count)
    block_size = blocks.shape[2]
    row_blocks = node_count // block_size
    fourier = fourier_basis(harmonics)
    samples = jnp.dot(fourier, field, preferred_element_type=jnp.float32)
    weighted = (rad_coeff.astype(jnp.float32) * samples).astype(jnp.bfloat16)
    radiative = jnp.dot(fourier.T, weighted, preferred_element_type=jnp.float32)
    rate_term = derivative_term(field.astype(jnp.float32))
    padded = with_halo(field, ((("harm", "node"), 1),), node_count)
    position = lax.axis_index(("harm", "node"))
    local_cols = block_cols - (position - 1) * row_blocks
    extended = padded.reshape(harmonics, 3 * row_blocks, block_size)
    gathered = jnp.take(extended, local_cols, axis=1)
    conduction = jnp.einsum(
        "kbsj,bsij->kbi", gathered, blocks, preferred_element_type=jnp.float32
    ).reshape(harmonics, node_count)
    residual = source - (capacity[None, :] * rate_term + conduction + radiative)
    updated = (field.astype(jnp.float32) + inv_diag[None, :] * residual).astype(jnp.bfloat16)
    returned = lax.all_to_all(
        updated.reshape(harmonics, 1, node_count), "harm", split_axis=0, concat_axis=1, tiled=True
    )
    weighted_terms = (updated.astype(jnp.float32) * heater_weight[None, :]).T
    window_zone = zone_of - (position - 1) * ZONE_DEV
    selector = (window_zone[:, None] == jnp.arange(3 * ZONE_DEV, dtype=jnp.int32)[None, :]).astype(
        jnp.float32
    )
    window_sums = jnp.einsum("nz,nk->zk", selector, weighted_terms, precision=lax.Precision.HIGHEST)
    lower_part = window_sums[:ZONE_DEV]
    middle_part = window_sums[ZONE_DEV : 2 * ZONE_DEV]
    upper_part = window_sums[2 * ZONE_DEV :]
    above_terms = passed_along(lower_part, ("harm", "node"), -1)
    below_terms = passed_along(upper_part, ("harm", "node"), 1)
    gradient = middle_part + above_terms + below_terms
    return (returned, gradient)


def solution(mesh):
    in_specs = (
        P("harm", None, "node"),
        P(None, ("harm", "node")),
        P(None, ("harm", "node")),
        P(("harm", "node")),
        P(("harm", "node")),
        P(("harm", "node"), None, None, None),
        P(("harm", "node"), None),
        P(("harm", "node")),
        P(("harm", "node")),
    )
    out_specs = (P("harm", None, "node"), P(("harm", "node"), None))
    return jax.shard_map(body, mesh=mesh, in_specs=in_specs, out_specs=out_specs, check_vma=False)
```

profile of v0, /device:TPU:4, one launch (start us, length us, event | category | flops | bytes accessed | tf_op | source)
XLA Modules:
  0.0 116.6 jit_solution(15993468261064862405)
XLA Ops:
  0.6 2.8 %copy.35 = bf16[32,4,4096]{2,0,1:T(8,128)(2,1)} copy(bf16[32,4,4096]{2,1,0:T(4,128)(2,1)} %param.9) | data formatting | bytes 2097152 | tf_op args[0]
  3.4 4.9 %all-to-all-start = ((bf16[32,4,4096]{2,0,1:T(8,128)(2,1)}), bf16[32,4,4096]{2,0,1:T(8,128)(2,1)S(1)}, u32[]{:S(2)}, u32[]{:S(2)}) async-start(bf16[32,4,4096]{2,0,1:T(8,128)(2,1)} %copy.35), calls=%async_computation | async-start | bytes 2097152 | tf_op jit(solution)/shard_map/all_to_all | solution.py:58
  8.5 0.1 copy.36
  8.6 25.4 %all-to-all-done = bf16[32,4,4096]{2,0,1:T(8,128)(2,1)S(1)} async-done(((bf16[32,4,4096]{2,0,1:T(8,128)(2,1)}), bf16[32,4,4096]{2,0,1:T(8,128)(2,1)S(1)}, u32[]{:S(2)}, u32[]{:S(2)}) %all-to-all-start) | async-done | bytes 1048608 | tf_op jit(solution)/shard_map/all_to_all | solution.py:58
  34.0 2.0 %collective-permute-start.1 = (bf16[128,4096]{1,0:T(8,128)(2,1)S(1)}, bf16[128,4096]{1,0:T(8,128)(2,1)S(1)}, u32[]{:S(2)}, u32[]{:S(2)}) collective-permute-start(bf16[128,4096]{1,0:T(8,128)(2,1)S(1)} %bitcast.39), channel_id=1, source_target_pairs={{1,0},{2,1},{3,2},{4,3},{5,4},{6,5},{7,6},{8,7},{9,8},{10,9},{11,1... | collective-permute-start | bytes 3145736 | tf_op jit(solution)/shard_map/ppermute | solution.py:18
  36.0 2.3 %collective-permute-start = (bf16[128,4096]{1,0:T(8,128)(2,1)S(1)}, bf16[128,4096]{1,0:T(8,128)(2,1)S(1)}, u32[]{:S(2)}, u32[]{:S(2)}) collective-permute-start(bf16[128,4096]{1,0:T(8,128)(2,1)S(1)} %bitcast.40), channel_id=1, source_target_pairs={{0,1},{1,2},{2,3},{3,4},{4,5},{5,6},{6,7},{7,8},{8,9},{9,10},{10,1... | collective-permute-start | bytes 3145736 | tf_op jit(solution)/shard_map/ppermute | solution.py:17
  38.3 0.3 bitcast_convert_fusion
  38.6 0.2 copy.48
  38.9 0.4 copy.38
  39.3 1.6 %slice_multiply_fusion.1 = (f32[63,4096]{1,0:T(8,128)}, f32[63,4096]{1,0:T(8,128)}) fusion(f32[128,4096]{1,0:T(8,128)S(1)} %bitcast_convert_fusion, f32[63]{0:T(128)S(1)} %get-tuple-element.10, f32[63]{0:T(128)S(1)} %get-tuple-element.11), kind=kLoop, calls=%fused_computation.24 | loop fusion | flops 516096 | bytes 4129272 | tf_op jit(solution)/shard_map/mul | solution.py:50
  40.9 15.8 %collective-permute-done.1 = bf16[128,4096]{1,0:T(8,128)(2,1)S(1)} collective-permute-done((bf16[128,4096]{1,0:T(8,128)(2,1)S(1)}, bf16[128,4096]{1,0:T(8,128)(2,1)S(1)}, u32[]{:S(2)}, u32[]{:S(2)}) %collective-permute-start.1) | collective-permute-done | bytes 1048608 | tf_op jit(solution)/shard_map/ppermute | solution.py:18
  56.7 0.3 copy_bitcast_fusion
  57.0 4.3 %collective-permute-done = bf16[128,4096]{1,0:T(8,128)(2,1)S(1)} collective-permute-done((bf16[128,4096]{1,0:T(8,128)(2,1)S(1)}, bf16[128,4096]{1,0:T(8,128)(2,1)S(1)}, u32[]{:S(2)}, u32[]{:S(2)}) %collective-permute-start) | collective-permute-done | bytes 1048608 | tf_op jit(solution)/shard_map/ppermute | solution.py:17
  61.4 0.3 copy_bitcast_fusion.1
  61.6 0.4 pad_maximum_fusion
  62.0 3.0 %gather_fusion = bf16[128,128,128]{2,1,0:T(8,128)(2,1)} fusion(bf16[128,96,128]{2,0,1:T(8,128)(2,1)S(1)} %pad_maximum_fusion, s32[1024]{0:T(1024)S(1)} %pad_clamp_fusion), kind=kCustom, calls=%fused_computation | custom fusion | bytes 8389120 | tf_op jit(solution)/shard_map/jit(_take)/gather | solution.py:73
  65.1 6.2 %fusion.5 = f32[32,128,128,1]{1,2,3,0:T(8,128)} fusion(bf16[32,4,128,128]{3,2,1,0:T(8,128)(2,1)} %param.14, bf16[32,4,128,128]{3,2,1,0:T(8,128)(2,1)} %bitcast.44, pred[32,4]{1,0:T(8,128)(4,1)S(1)} %copy.36), kind=kOutput, calls=%fused_computation.8 | convolution fusion | flops 538968064 | bytes 10485888 | tf_op jit(solution)/shard_map/kbsj,bsij->kbi/dot_general | solution.py:74
  71.3 2.0 %copy.41 = f32[128,4096]{1,0:T(8,128)S(1)} copy(f32[128,4096]{0,1:T(8,128)} %bitcast.47) | data formatting | bytes 4194304 | tf_op jit(solution)/shard_map/reshape | solution.py:76
  73.3 5.2 %fusion.4 = bf16[128,4096]{1,0:T(8,128)(2,1)} fusion(f32[128,4096]{1,0:T(8,128)} %param.10, f32[128,4096]{1,0:T(8,128)S(1)} %copy.41, f32[63,4096]{1,0:T(8,128)} %get-tuple-element.7, f32[1,4096]{1,0:T(1,128)S(1)} %broadcast_in_dim.41, f32[63,4096]{1,0:T(8,128)} %get-tuple-element.6, bf16[128,4096]{1,0:T(8,128)(2,1)S(1)} %bitcast.42, ...), kind=kOutput, calls=%fused_computation.7 | convolution fusion | flops 275939328 | bytes 9454720 | tf_op jit(solution)/shard_map/dot_general | solution.py:67
  78.5 0.5 broadcast.81
  79.0 2.6 %reduce = bf16[128,4096]{1,0:T(8,128)(2,1)S(1)} reduce(bf16[128,1,4096]{2,0,1:T(8,128)(2,1)} %bitcast.46, bf16[]{:T(256)} %broadcast.81), dimensions={1}, to_apply=%copy.42.reduce_sub_computation | reduce | bytes 2097154 | tf_op jit(solution)/shard_map/reshape | solution.py:80
  81.7 2.0 %reshape.81 = bf16[4,2,65536]{2,1,0:T(2,128)(2,1)} reshape(bf16[128,4096]{1,0:T(8,128)(2,1)S(1)} %reduce) | data formatting | bytes 2097152
  83.7 3.5 %all-to-all-start.1 = ((bf16[4,2,65536]{2,1,0:T(2,128)(2,1)}), bf16[4,2,65536]{2,1,0:T(2,128)(2,1)S(1)}, u32[]{:S(2)}, u32[]{:S(2)}) async-start(bf16[4,2,65536]{2,1,0:T(2,128)(2,1)} %reshape.81), calls=%async_computation.1 | async-start | bytes 2097152 | tf_op jit(solution)/shard_map/all_to_all | solution.py:79
  87.3 2.1 %fusion.11 = f32[120,128]{1,0:T(8,128)S(1)} fusion(bf16[128,4096]{1,0:T(8,128)(2,1)S(1)} %copy-done.2, f32[4096]{0:T(1024)S(1)} %copy-done.7, s32[4096]{0:T(1024)S(1)} %broadcast_subtract_fusion), kind=kOutput, calls=%fused_computation.16 | convolution fusion | flops 757006336 | bytes 1142784 | tf_op jit(solution)/shard_map/nz,nk->zk/dot_general | solution.py:87
  89.4 1.9 %collective-permute-start.2 = (f32[40,128]{1,0:T(8,128)S(1)}, f32[40,128]{1,0:T(8,128)S(1)}, u32[]{:S(2)}, u32[]{:S(2)}) collective-permute-start(f32[40,128]{1,0:T(8,128)S(1)} %get-tuple-element.8), channel_id=1, source_target_pairs={{1,0},{2,1},{3,2},{4,3},{5,4},{6,5},{7,6},{8,7},{9,8},{10,9},{11,1... | collective-permute-start | bytes 61448 | tf_op jit(solution)/shard_map/ppermute | solution.py:26
  91.3 2.4 %collective-permute-start.3 = (f32[40,128]{1,0:T(8,128)S(1)}, f32[40,128]{1,0:T(8,128)S(1)}, u32[]{:S(2)}, u32[]{:S(2)}) collective-permute-start(f32[40,128]{1,0:T(8,128)S(1)} %get-tuple-element.9), channel_id=1, source_target_pairs={{0,1},{1,2},{2,3},{3,4},{4,5},{5,6},{6,7},{7,8},{8,9},{9,10},{10,1... | collective-permute-start | bytes 61448 | tf_op jit(solution)/shard_map/ppermute | solution.py:26
  93.7 3.6 %collective-permute-done.3 = f32[40,128]{1,0:T(8,128)S(1)} collective-permute-done((f32[40,128]{1,0:T(8,128)S(1)}, f32[40,128]{1,0:T(8,128)S(1)}, u32[]{:S(2)}, u32[]{:S(2)}) %collective-permute-start.3) | collective-permute-done | bytes 20512 | tf_op jit(solution)/shard_map/ppermute | solution.py:26
  97.3 0.6 fusion.26
  97.9 14.8 %all-to-all-done.1 = bf16[4,2,65536]{2,1,0:T(2,128)(2,1)S(1)} async-done(((bf16[4,2,65536]{2,1,0:T(2,128)(2,1)}), bf16[4,2,65536]{2,1,0:T(2,128)(2,1)S(1)}, u32[]{:S(2)}, u32[]{:S(2)}) %all-to-all-start.1) | async-done | bytes 1048608 | tf_op jit(solution)/shard_map/all_to_all | solution.py:79
  112.7 0.9 reshape.82
  113.7 1.1 copy.45
  114.9 1.8 %copy.43 = bf16[32,4,4096]{2,1,0:T(4,128)(2,1)} copy(bf16[32,4,4096]{2,0,1:T(8,128)(2,1)S(1)} %bitcast.43) | data formatting | bytes 2097152
  (27 shorter events, 0.3 us)
Async XLA Ops:
  0.6 7.7 %copy-start.6 = (s32[32,4]{0,1:T(4,128)S(1)}, s32[32,4]{0,1:T(4,128)}, u32[]{:S(2)}) copy-start(s32[32,4]{0,1:T(4,128)} %param.15) | copy-start | bytes 1540
  3.4 30.6 %all-to-all-start = ((bf16[32,4,4096]{2,0,1:T(8,128)(2,1)}), bf16[32,4,4096]{2,0,1:T(8,128)(2,1)S(1)}, u32[]{:S(2)}, u32[]{:S(2)}) async-start(bf16[32,4,4096]{2,0,1:T(8,128)(2,1)} %copy.35), calls=%async_computation | async-start | bytes 2097152 | tf_op jit(solution)/shard_map/all_to_all | solution.py:58
  34.0 4.9 %copy-start = (bf16[32,4,4096]{2,0,1:T(8,128)(2,1)}, bf16[32,4,4096]{2,0,1:T(8,128)(2,1)S(1)}, u32[]{:S(2)}) copy-start(bf16[32,4,4096]{2,0,1:T(8,128)(2,1)S(1)} %all-to-all-done) | copy-start | bytes 3145732
  34.0 22.7 %collective-permute-start.1 = (bf16[128,4096]{1,0:T(8,128)(2,1)S(1)}, bf16[128,4096]{1,0:T(8,128)(2,1)S(1)}, u32[]{:S(2)}, u32[]{:S(2)}) collective-permute-start(bf16[128,4096]{1,0:T(8,128)(2,1)S(1)} %bitcast.39), channel_id=1, source_target_pairs={{1,0},{2,1},{3,2},{4,3},{5,4},{6,5},{7,6},{8,7},{9,8},{10,9},{11,1... | collective-permute-start | bytes 3145736 | tf_op jit(solution)/shard_map/ppermute | solution.py:18
  36.0 25.3 %collective-permute-start = (bf16[128,4096]{1,0:T(8,128)(2,1)S(1)}, bf16[128,4096]{1,0:T(8,128)(2,1)S(1)}, u32[]{:S(2)}, u32[]{:S(2)}) collective-permute-start(bf16[128,4096]{1,0:T(8,128)(2,1)S(1)} %bitcast.40), channel_id=1, source_target_pairs={{0,1},{1,2},{2,3},{3,4},{4,5},{5,6},{6,7},{7,8},{8,9},{9,10},{10,1... | collective-permute-start | bytes 3145736 | tf_op jit(solution)/shard_map/ppermute | solution.py:17
  71.3 2.0 %copy-start.1 = (bf16[32,4,4096]{2,0,1:T(8,128)(2,1)S(1)}, bf16[32,4,4096]{2,0,1:T(8,128)(2,1)}, u32[]{:S(2)}) copy-start(bf16[32,4,4096]{2,0,1:T(8,128)(2,1)} %copy-done) | copy-start | bytes 3145732
  71.3 2.0 %copy-start.3 = (f32[4096]{0:T(1024)S(1)}, f32[4096]{0:T(1024)}, u32[]{:S(2)}) copy-start(f32[4096]{0:T(1024)} %param.12) | copy-start | bytes 49156
  71.3 2.1 %copy-start.4 = (f32[4096]{0:T(1024)S(1)}, f32[4096]{0:T(1024)}, u32[]{:S(2)}) copy-start(f32[4096]{0:T(1024)} %param.13) | copy-start | bytes 49156
  81.7 5.6 %copy-start.5 = (s32[4096]{0:T(1024)S(1)}, s32[4096]{0:T(1024)}, u32[]{:S(2)}) copy-start(s32[4096]{0:T(1024)} %param.16) | copy-start | bytes 49156
  81.7 5.6 %copy-start.2 = (bf16[128,4096]{1,0:T(8,128)(2,1)S(1)}, bf16[128,4096]{1,0:T(8,128)(2,1)}, u32[]{:S(2)}) copy-start(bf16[128,4096]{1,0:T(8,128)(2,1)} %fusion.4) | copy-start | bytes 3145732
  81.7 5.6 %copy-start.7 = (f32[4096]{0:T(1024)S(1)}, f32[4096]{0:T(1024)}, u32[]{:S(2)}) copy-start(f32[4096]{0:T(1024)} %param.17) | copy-start | bytes 49156
  83.7 29.0 %all-to-all-start.1 = ((bf16[4,2,65536]{2,1,0:T(2,128)(2,1)}), bf16[4,2,65536]{2,1,0:T(2,128)(2,1)S(1)}, u32[]{:S(2)}, u32[]{:S(2)}) async-start(bf16[4,2,65536]{2,1,0:T(2,128)(2,1)} %reshape.81), calls=%async_computation.1 | async-start | bytes 2097152 | tf_op jit(solution)/shard_map/all_to_all | solution.py:79
  89.4 4.3 %collective-permute-start.2 = (f32[40,128]{1,0:T(8,128)S(1)}, f32[40,128]{1,0:T(8,128)S(1)}, u32[]{:S(2)}, u32[]{:S(2)}) collective-permute-start(f32[40,128]{1,0:T(8,128)S(1)} %get-tuple-element.8), channel_id=1, source_target_pairs={{1,0},{2,1},{3,2},{4,3},{5,4},{6,5},{7,6},{8,7},{9,8},{10,9},{11,1... | collective-permute-start | bytes 61448 | tf_op jit(solution)/shard_map/ppermute | solution.py:26
  91.3 6.0 %collective-permute-start.3 = (f32[40,128]{1,0:T(8,128)S(1)}, f32[40,128]{1,0:T(8,128)S(1)}, u32[]{:S(2)}, u32[]{:S(2)}) collective-permute-start(f32[40,128]{1,0:T(8,128)S(1)} %get-tuple-element.9), channel_id=1, source_target_pairs={{0,1},{1,2},{2,3},{3,4},{4,5},{5,6},{6,7},{7,8},{8,9},{9,10},{10,1... | collective-permute-start | bytes 61448 | tf_op jit(solution)/shard_map/ppermute | solution.py:26
where the time goes:
time: 117 us
  waiting for transfers between devices  63.9 us (55%)
  starting transfers between devices  17 us (15%)
  local copies, waits for them, and re-layouts  15.8 us (14%)
  matrix products  13.5 us (12%)
  other arithmetic  5.56 us (5%)
    all_to_all x1, waiting for transfers between devices, body(): lax.all_to_all(adjoint, 'harm', split_axis=1, concat_axis=0, tiled=True)  25.4 us
    ppermute x1, waiting for transfers between devices, with_halo(): after = lax.ppermute(initial, axis, down)  15.8 us
    all_to_all x1, waiting for transfers between devices, body(): lax.all_to_all(updated.reshape(harmonics, 1, node_count), 'harm', split_a...  14.8 us
    unnamed x22, local copies, waits for them, and re-layouts  8.93 us
    dot_general x1, matrix products, body(): jnp.einsum('kbsj,bsij->kbi', gathered, blocks, preferred_element_type=jnp...  6.17 us
    dot_general x1, matrix products, body(): radiative = jnp.dot(fourier.T, weighted, preferred_element_type=jnp.float32)  5.2 us
    all_to_all x1, starting transfers between devices, body(): lax.all_to_all(adjoint, 'harm', split_axis=1, concat_axis=0, tiled=True)  4.87 us
    ppermute x2, starting transfers between devices, passed_along(): lax.ppermute(value, axis, [(source, source + steps) for source in range(i...  4.33 us
  transfers between devices with their start and end apart: 6, of which 5 were waited for; matrix products, arithmetic and copies ran while one was open for 5% of the time, Pallas kernels for 0%

commit v1 on v0

--- a/solution.py
+++ b/solution.py
@@ -76,8 +76,17 @@
     ).reshape(harmonics, node_count)
     residual = source - (capacity[None, :] * rate_term + conduction + radiative)
     updated = (field.astype(jnp.float32) + inv_diag[None, :] * residual).astype(jnp.bfloat16)
-    returned = lax.all_to_all(
-        updated.reshape(harmonics, 1, node_count), "harm", split_axis=0, concat_axis=1, tiled=True
+    returned = jnp.concatenate(
+        lax.all_to_all(
+            jnp.stack(
+                jnp.split(updated.reshape(harmonics, 1, node_count), lax.axis_size("harm"), axis=0),
+                axis=0,
+            ),
+            "harm",
+            0,
+            0,
+        ),
+        axis=1,
     )
     weighted_terms = (updated.astype(jnp.float32) * heater_weight[None, :]).T
     window_zone = zone_of - (position - 1) * ZONE_DEV

time: 117 us -> 112 us (0.957)
  local copies, waits for them, and re-layouts: 15.8 us -> 12.4 us
  other arithmetic: 5.56 us -> 4.03 us
    unnamed x22 -> x19, local copies, waits for them, and re-layouts: 8.93 us -> 4.84 us
    reshape x1 -> x0, other arithmetic: 2.63 us -> none  [body(): updated.reshape(harmonics, 1, node_count)]
    another operation x0 -> x1, local copies, waits for them, and re-layouts: none -> 1.25 us  [body(): jnp.stack(jnp.split(updated.reshape(harmonics, 1, node_count), lax.axis_s...]
where the time goes in v1:
time: 112 us
  waiting for transfers between devices  63.9 us (57%)
  starting transfers between devices  17 us (15%)
  matrix products  13.5 us (12%)
  local copies, waits for them, and re-layouts  12.4 us (11%)
  other arithmetic  4.03 us (4%)
    all_to_all x1, waiting for transfers between devices, body(): lax.all_to_all(adjoint, 'harm', split_axis=1, concat_axis=0, tiled=True)  25.4 us
    ppermute x1, waiting for transfers between devices, with_halo(): after = lax.ppermute(initial, axis, down)  15.8 us
    all_to_all x1, waiting for transfers between devices, body(): lax.all_to_all(jnp.stack(jnp.split(updated.reshape(harmonics, 1, node_cou...  14.8 us
    dot_general x1, matrix products, body(): jnp.einsum('kbsj,bsij->kbi', gathered, blocks, preferred_element_type=jnp...  6.15 us
    dot_general x1, matrix products, body(): radiative = jnp.dot(fourier.T, weighted, preferred_element_type=jnp.float32)  5.21 us
    all_to_all x1, starting transfers between devices, body(): lax.all_to_all(adjoint, 'harm', split_axis=1, concat_axis=0, tiled=True)  4.87 us
    unnamed x19, local copies, waits for them, and re-layouts  4.84 us
    ppermute x2, starting transfers between devices, passed_along(): lax.ppermute(value, axis, [(source, source + steps) for source in range(i...  4.33 us
  transfers between devices with their start and end apart: 6, of which 5 were waited for; matrix products, arithmetic and copies ran while one was open for 5% of the time, Pallas kernels for 0%

profile of v1, /device:TPU:4, one launch (start us, length us, event | category | flops | bytes accessed | tf_op | source)
XLA Modules:
  0.0 111.7 jit_solution(12471242795779360121)
XLA Ops:
  0.6 2.8 %copy.26 = bf16[32,4,4096]{2,0,1:T(8,128)(2,1)} copy(bf16[32,4,4096]{2,1,0:T(4,128)(2,1)} %param.9) | data formatting | bytes 2097152 | tf_op args[0]
  3.4 4.9 %all-to-all-start = ((bf16[32,4,4096]{2,0,1:T(8,128)(2,1)}), bf16[32,4,4096]{2,0,1:T(8,128)(2,1)S(1)}, u32[]{:S(2)}, u32[]{:S(2)}) async-start(bf16[32,4,4096]{2,0,1:T(8,128)(2,1)} %copy.26), calls=%async_computation | async-start | bytes 2097152 | tf_op jit(solution)/shard_map/all_to_all | solution.py:58
  8.3 0.1 copy.31
  8.4 0.1 reshape.85
  8.5 0.1 copy.27
  8.6 25.4 %all-to-all-done = bf16[32,4,4096]{2,0,1:T(8,128)(2,1)S(1)} async-done(((bf16[32,4,4096]{2,0,1:T(8,128)(2,1)}), bf16[32,4,4096]{2,0,1:T(8,128)(2,1)S(1)}, u32[]{:S(2)}, u32[]{:S(2)}) %all-to-all-start) | async-done | bytes 1048608 | tf_op jit(solution)/shard_map/all_to_all | solution.py:58
  34.0 2.0 %collective-permute-start.1 = (bf16[128,4096]{1,0:T(8,128)(2,1)S(1)}, bf16[128,4096]{1,0:T(8,128)(2,1)S(1)}, u32[]{:S(2)}, u32[]{:S(2)}) collective-permute-start(bf16[128,4096]{1,0:T(8,128)(2,1)S(1)} %bitcast.44), channel_id=1, source_target_pairs={{1,0},{2,1},{3,2},{4,3},{5,4},{6,5},{7,6},{8,7},{9,8},{10,9},{11,1... | collective-permute-start | bytes 3145736 | tf_op jit(solution)/shard_map/ppermute | solution.py:18
  36.0 2.3 %collective-permute-start = (bf16[128,4096]{1,0:T(8,128)(2,1)S(1)}, bf16[128,4096]{1,0:T(8,128)(2,1)S(1)}, u32[]{:S(2)}, u32[]{:S(2)}) collective-permute-start(bf16[128,4096]{1,0:T(8,128)(2,1)S(1)} %bitcast.45), channel_id=1, source_target_pairs={{0,1},{1,2},{2,3},{3,4},{4,5},{5,6},{6,7},{7,8},{8,9},{9,10},{10,1... | collective-permute-start | bytes 3145736 | tf_op jit(solution)/shard_map/ppermute | solution.py:17
  38.3 0.3 bitcast_convert_fusion
  38.6 0.2 copy.37
  38.9 0.4 copy.29
  39.3 1.6 %slice_multiply_fusion.1 = (f32[63,4096]{1,0:T(8,128)}, f32[63,4096]{1,0:T(8,128)}) fusion(f32[128,4096]{1,0:T(8,128)S(1)} %bitcast_convert_fusion, f32[63]{0:T(128)S(1)} %get-tuple-element.18, f32[63]{0:T(128)S(1)} %get-tuple-element.19), kind=kLoop, calls=%fused_computation.24 | loop fusion | flops 516096 | bytes 4129272 | tf_op jit(solution)/shard_map/mul | solution.py:50
  40.9 15.8 %collective-permute-done.1 = bf16[128,4096]{1,0:T(8,128)(2,1)S(1)} collective-permute-done((bf16[128,4096]{1,0:T(8,128)(2,1)S(1)}, bf16[128,4096]{1,0:T(8,128)(2,1)S(1)}, u32[]{:S(2)}, u32[]{:S(2)}) %collective-permute-start.1) | collective-permute-done | bytes 1048608 | tf_op jit(solution)/shard_map/ppermute | solution.py:18
  56.7 0.3 copy_bitcast_fusion
  57.0 4.3 %collective-permute-done = bf16[128,4096]{1,0:T(8,128)(2,1)S(1)} collective-permute-done((bf16[128,4096]{1,0:T(8,128)(2,1)S(1)}, bf16[128,4096]{1,0:T(8,128)(2,1)S(1)}, u32[]{:S(2)}, u32[]{:S(2)}) %collective-permute-start) | collective-permute-done | bytes 1048608 | tf_op jit(solution)/shard_map/ppermute | solution.py:17
  61.4 0.3 copy_bitcast_fusion.1
  61.6 0.4 pad_maximum_fusion
  62.0 3.0 %gather_fusion = bf16[128,128,128]{2,1,0:T(8,128)(2,1)} fusion(bf16[128,96,128]{2,0,1:T(8,128)(2,1)S(1)} %pad_maximum_fusion, s32[1024]{0:T(1024)S(1)} %pad_clamp_fusion), kind=kCustom, calls=%fused_computation | custom fusion | bytes 8389120 | tf_op jit(solution)/shard_map/jit(_take)/gather | solution.py:73
  65.1 6.2 %fusion.5 = f32[32,128,128,1]{1,2,3,0:T(8,128)} fusion(bf16[32,4,128,128]{3,2,1,0:T(8,128)(2,1)} %param.14, bf16[32,4,128,128]{3,2,1,0:T(8,128)(2,1)} %bitcast.48, pred[32,4]{1,0:T(8,128)(4,1)S(1)} %copy.27), kind=kOutput, calls=%fused_computation.8 | convolution fusion | flops 538968064 | bytes 10485888 | tf_op jit(solution)/shard_map/kbsj,bsij->kbi/dot_general | solution.py:74
  71.2 2.0 %copy.32 = f32[128,4096]{1,0:T(8,128)S(1)} copy(f32[128,4096]{0,1:T(8,128)} %bitcast.51) | data formatting | bytes 4194304 | tf_op jit(solution)/shard_map/reshape | solution.py:76
  73.3 5.2 %fusion.4 = bf16[128,4096]{1,0:T(8,128)(2,1)} fusion(f32[128,4096]{1,0:T(8,128)} %param.10, f32[128,4096]{1,0:T(8,128)S(1)} %copy.32, f32[63,4096]{1,0:T(8,128)} %get-tuple-element.11, f32[1,4096]{1,0:T(1,128)S(1)} %broadcast_in_dim.41, f32[63,4096]{1,0:T(8,128)} %get-tuple-element.10, bf16[128,4096]{1,0:T(8,128)(2,1)S(1)} %bitcast.47, ...), kind=kOutput, calls=%fused_computation.7 | convolution fusion | flops 275939328 | bytes 9454720 | tf_op jit(solution)/shard_map/dot_general | solution.py:67
  78.5 1.3 %slice_bitcast_fusion.3 = (bf16[1,32,1,4096]{3,1,2,0:T(8,128)(2,1)S(1)}, bf16[1,32,1,4096]{3,1,2,0:T(8,128)(2,1)S(1)}, bf16[1,32,1,4096]{3,1,2,0:T(8,128)(2,1)S(1)}, bf16[1,32,1,4096]{3,1,2,0:T(8,128)(2,1)S(1)}) fusion(bf16[128,4096]{1,0:T(8,128)(2,1)} %fusion.4), kind=kLoop, calls=%fused_computation.31 | loop fusion | bytes 2097152 | tf_op jit(solution)/shard_map/stack | solution.py:81
  79.8 0.0 copy-start.5
  79.8 1.1 pad_maximum_fusion.1
  80.9 3.5 %all-to-all-start.1 = ((bf16[4,32,1,4096]{3,1,2,0:T(8,128)(2,1)}), bf16[4,32,1,4096]{3,1,2,0:T(8,128)(2,1)S(1)}, u32[]{:S(2)}, u32[]{:S(2)}) async-start(bf16[4,32,1,4096]{3,1,2,0:T(8,128)(2,1)} %pad_maximum_fusion.1), calls=%async_computation.1 | async-start | bytes 2097152 | tf_op jit(solution)/shard_map/all_to_all | solution.py:80
  84.5 2.1 %fusion.11 = f32[120,128]{1,0:T(8,128)S(1)} fusion(bf16[128,4096]{1,0:T(8,128)(2,1)S(1)} %copy-done.2, f32[4096]{0:T(1024)S(1)} %copy-done.7, s32[4096]{0:T(1024)S(1)} %broadcast_subtract_fusion), kind=kOutput, calls=%fused_computation.16 | convolution fusion | flops 757006336 | bytes 1142784 | tf_op jit(solution)/shard_map/nz,nk->zk/dot_general | solution.py:96
  86.6 1.9 %collective-permute-start.2 = (f32[40,128]{1,0:T(8,128)S(1)}, f32[40,128]{1,0:T(8,128)S(1)}, u32[]{:S(2)}, u32[]{:S(2)}) collective-permute-start(f32[40,128]{1,0:T(8,128)S(1)} %get-tuple-element.16), channel_id=1, source_target_pairs={{1,0},{2,1},{3,2},{4,3},{5,4},{6,5},{7,6},{8,7},{9,8},{10,9},{11,1... | collective-permute-start | bytes 61448 | tf_op jit(solution)/shard_map/ppermute | solution.py:26
  88.5 2.4 %collective-permute-start.3 = (f32[40,128]{1,0:T(8,128)S(1)}, f32[40,128]{1,0:T(8,128)S(1)}, u32[]{:S(2)}, u32[]{:S(2)}) collective-permute-start(f32[40,128]{1,0:T(8,128)S(1)} %get-tuple-element.17), channel_id=1, source_target_pairs={{0,1},{1,2},{2,3},{3,4},{4,5},{5,6},{6,7},{7,8},{8,9},{9,10},{10,1... | collective-permute-start | bytes 61448 | tf_op jit(solution)/shard_map/ppermute | solution.py:26
  90.9 3.6 %collective-permute-done.3 = f32[40,128]{1,0:T(8,128)S(1)} collective-permute-done((f32[40,128]{1,0:T(8,128)S(1)}, f32[40,128]{1,0:T(8,128)S(1)}, u32[]{:S(2)}, u32[]{:S(2)}) %collective-permute-start.3) | collective-permute-done | bytes 20512 | tf_op jit(solution)/shard_map/ppermute | solution.py:26
  94.5 0.6 fusion.26
  95.1 14.8 %all-to-all-done.1 = bf16[4,32,1,4096]{3,1,2,0:T(8,128)(2,1)S(1)} async-done(((bf16[4,32,1,4096]{3,1,2,0:T(8,128)(2,1)}), bf16[4,32,1,4096]{3,1,2,0:T(8,128)(2,1)S(1)}, u32[]{:S(2)}, u32[]{:S(2)}) %all-to-all-start.1) | async-done | bytes 1048608 | tf_op jit(solution)/shard_map/all_to_all | solution.py:80
  109.9 1.8 %copy.33 = bf16[32,4,4096]{2,1,0:T(4,128)(2,1)} copy(bf16[32,4,4096]{2,0,1:T(8,128)(2,1)S(1)} %bitcast.49) | data formatting | bytes 2097152
  (24 shorter events, 0.1 us)
Async XLA Ops:
  0.6 7.7 %copy-start.6 = (s32[32,4]{0,1:T(4,128)S(1)}, s32[32,4]{0,1:T(4,128)}, u32[]{:S(2)}) copy-start(s32[32,4]{0,1:T(4,128)} %param.15) | copy-start | bytes 1540
  3.4 30.6 %all-to-all-start = ((bf16[32,4,4096]{2,0,1:T(8,128)(2,1)}), bf16[32,4,4096]{2,0,1:T(8,128)(2,1)S(1)}, u32[]{:S(2)}, u32[]{:S(2)}) async-start(bf16[32,4,4096]{2,0,1:T(8,128)(2,1)} %copy.26), calls=%async_computation | async-start | bytes 2097152 | tf_op jit(solution)/shard_map/all_to_all | solution.py:58
  34.0 4.9 %copy-start = (bf16[32,4,4096]{2,0,1:T(8,128)(2,1)}, bf16[32,4,4096]{2,0,1:T(8,128)(2,1)S(1)}, u32[]{:S(2)}) copy-start(bf16[32,4,4096]{2,0,1:T(8,128)(2,1)S(1)} %all-to-all-done) | copy-start | bytes 3145732
  34.0 22.7 %collective-permute-start.1 = (bf16[128,4096]{1,0:T(8,128)(2,1)S(1)}, bf16[128,4096]{1,0:T(8,128)(2,1)S(1)}, u32[]{:S(2)}, u32[]{:S(2)}) collective-permute-start(bf16[128,4096]{1,0:T(8,128)(2,1)S(1)} %bitcast.44), channel_id=1, source_target_pairs={{1,0},{2,1},{3,2},{4,3},{5,4},{6,5},{7,6},{8,7},{9,8},{10,9},{11,1... | collective-permute-start | bytes 3145736 | tf_op jit(solution)/shard_map/ppermute | solution.py:18
  36.0 25.3 %collective-permute-start = (bf16[128,4096]{1,0:T(8,128)(2,1)S(1)}, bf16[128,4096]{1,0:T(8,128)(2,1)S(1)}, u32[]{:S(2)}, u32[]{:S(2)}) collective-permute-start(bf16[128,4096]{1,0:T(8,128)(2,1)S(1)} %bitcast.45), channel_id=1, source_target_pairs={{0,1},{1,2},{2,3},{3,4},{4,5},{5,6},{6,7},{7,8},{8,9},{9,10},{10,1... | collective-permute-start | bytes 3145736 | tf_op jit(solution)/shard_map/ppermute | solution.py:17
  71.2 2.0 %copy-start.1 = (bf16[32,4,4096]{2,0,1:T(8,128)(2,1)S(1)}, bf16[32,4,4096]{2,0,1:T(8,128)(2,1)}, u32[]{:S(2)}) copy-start(bf16[32,4,4096]{2,0,1:T(8,128)(2,1)} %copy-done) | copy-start | bytes 3145732
  71.2 2.0 %copy-start.3 = (f32[4096]{0:T(1024)S(1)}, f32[4096]{0:T(1024)}, u32[]{:S(2)}) copy-start(f32[4096]{0:T(1024)} %param.12) | copy-start | bytes 49156
  71.2 2.1 %copy-start.4 = (f32[4096]{0:T(1024)S(1)}, f32[4096]{0:T(1024)}, u32[]{:S(2)}) copy-start(f32[4096]{0:T(1024)} %param.13) | copy-start | bytes 49156
  79.8 4.7 %copy-start.5 = (s32[4096]{0:T(1024)S(1)}, s32[4096]{0:T(1024)}, u32[]{:S(2)}) copy-start(s32[4096]{0:T(1024)} %param.16) | copy-start | bytes 49156
  79.8 4.7 %copy-start.2 = (bf16[128,4096]{1,0:T(8,128)(2,1)S(1)}, bf16[128,4096]{1,0:T(8,128)(2,1)}, u32[]{:S(2)}) copy-start(bf16[128,4096]{1,0:T(8,128)(2,1)} %fusion.4) | copy-start | bytes 3145732
  79.8 4.7 %copy-start.7 = (f32[4096]{0:T(1024)S(1)}, f32[4096]{0:T(1024)}, u32[]{:S(2)}) copy-start(f32[4096]{0:T(1024)} %param.17) | copy-start | bytes 49156
  80.9 29.0 %all-to-all-start.1 = ((bf16[4,32,1,4096]{3,1,2,0:T(8,128)(2,1)}), bf16[4,32,1,4096]{3,1,2,0:T(8,128)(2,1)S(1)}, u32[]{:S(2)}, u32[]{:S(2)}) async-start(bf16[4,32,1,4096]{3,1,2,0:T(8,128)(2,1)} %pad_maximum_fusion.1), calls=%async_computation.1 | async-start | bytes 2097152 | tf_op jit(solution)/shard_map/all_to_all | solution.py:80
  86.6 4.3 %collective-permute-start.2 = (f32[40,128]{1,0:T(8,128)S(1)}, f32[40,128]{1,0:T(8,128)S(1)}, u32[]{:S(2)}, u32[]{:S(2)}) collective-permute-start(f32[40,128]{1,0:T(8,128)S(1)} %get-tuple-element.16), channel_id=1, source_target_pairs={{1,0},{2,1},{3,2},{4,3},{5,4},{6,5},{7,6},{8,7},{9,8},{10,9},{11,1... | collective-permute-start | bytes 61448 | tf_op jit(solution)/shard_map/ppermute | solution.py:26
  88.5 6.0 %collective-permute-start.3 = (f32[40,128]{1,0:T(8,128)S(1)}, f32[40,128]{1,0:T(8,128)S(1)}, u32[]{:S(2)}, u32[]{:S(2)}) collective-permute-start(f32[40,128]{1,0:T(8,128)S(1)} %get-tuple-element.17), channel_id=1, source_target_pairs={{0,1},{1,2},{2,3},{3,4},{4,5},{5,6},{6,7},{7,8},{8,9},{9,10},{10,1... | collective-permute-start | bytes 61448 | tf_op jit(solution)/shard_map/ppermute | solution.py:26
